TPU v7x, 256 devices: a whole 4x4x8 slice. The times are simulated.
256 devices in a mesh: rep: 32 (over x, z_lo, core), fsdp: 8 (over z_hi, y).
Axes of the slice: x: 4, y: 4, z: 8 (z_hi: 2, z_lo: 4; z = z_hi * 4 + z_lo), core: 2. Of those that a mesh axis runs over, the one named last changes fastest.
Arguments:
- tokens: bfloat16 [49152, 5120], P(('rep', 'fsdp')), may hold values from -6 to 6
- cotangent: bfloat16 [49152, 2560], P(('rep', 'fsdp')), may hold values from -0.15625 to 0.15625
- momentum: bfloat16 [32, 5120, 2560], P('rep', 'fsdp'), may hold values from -6 to 6
- positions: int32 [5120, 320], P('fsdp'), may hold values from 0 to 63, as said below
Outputs:
- new_momentum: bfloat16 [32, 5120, 2560], P('rep', 'fsdp')
- update: bfloat16 [5120, 2560], P(('fsdp', 'rep'))
Inputs may be any that keep to these rules, and one draw needn't show every extreme that they name: The 8 positions of each block are distinct; the same positions hold for every replica.
All inputs are finite; a program needn't handle non-finite values.
Results may differ from a plain program's by a relative error of at most 0.015.
Values may be sent and summed in bfloat16 or wider, within the bound.
A program may use at most 128 MiB of HBM per device.

v0:
```python
import math

import jax
import jax.numpy as jnp
from jax import lax
from jax.sharding import PartitionSpec as P

SPAN = 64
KEEP = 8


momentum_decay = 0.9


def dct_basis(length):
    freqs = jnp.arange(length, dtype=jnp.float32)[:, None]
    places = jnp.arange(length, dtype=jnp.float32)[None, :]
    weights = jnp.where(freqs == 0.0, math.sqrt(1.0 / length), math.sqrt(2.0 / length))
    return weights * jnp.cos(math.pi * (2.0 * places + 1.0) * freqs / (2.0 * length))


def selection(slots, length, keep):
    rows = slots.shape[0]
    grouped = slots.reshape(rows, -1, keep)
    return grouped[..., None] == jnp.arange(length, dtype=jnp.int32)


def expand(values, chosen, basis):
    spread = jnp.sum(jnp.where(chosen, values[..., None], 0.0), axis=2)
    return jnp.einsum("rck,kj->rcj", spread, basis, precision=lax.Precision.HIGHEST)


def compress(updated, slots, basis, keep):
    rows, width = updated.shape
    length = basis.shape[0]
    spans = updated.reshape(rows, width // length, length)
    coeffs = jnp.einsum("rcj,kj->rck", spans, basis, precision=lax.Precision.HIGHEST)
    chosen = selection(slots, length, keep)
    values = jnp.sum(jnp.where(chosen, coeffs[:, :, None, :], 0.0), axis=3).astype(jnp.bfloat16)
    restored = expand(values.astype(jnp.float32), chosen, basis)
    leftover = (spans - restored).reshape(rows, width).astype(jnp.bfloat16)
    return (values.reshape(rows, -1), leftover)


def decode(summed, slots, basis, keep, factor):
    rows = summed.shape[0]
    length = basis.shape[0]
    chosen = selection(slots, length, keep)
    restored = expand(summed.reshape(rows, -1, keep), chosen, basis)
    return (restored.reshape(rows, -1) * factor).astype(jnp.bfloat16)


def local(tokens, cotangent, momentum, positions):
    replicas = lax.axis_size("rep")
    rep_index = lax.axis_index("rep")
    columns = lax.all_to_all(tokens, "fsdp", split_axis=1, concat_axis=0, tiled=True)
    rows_here = columns.shape[1]
    width = cotangent.shape[1]
    gradient = lax.dot_general(
        columns,
        lax.all_gather(cotangent, "fsdp", axis=0, tiled=True),
        (((0,), (0,)), ((), ())),
        preferred_element_type=jnp.float32,
    )
    updated = momentum_decay * momentum[0].astype(jnp.float32) + gradient
    basis = dct_basis(SPAN)
    block_rows = math.gcd(rows_here, 64)
    block_count = rows_here // block_rows

    def compress_block(inputs):
        return compress(inputs[0], inputs[1], basis, KEEP)

    values, leftover = lax.map(
        compress_block,
        (
            updated.reshape(block_count, block_rows, width),
            positions.reshape(block_count, block_rows, -1),
        ),
    )
    values = values.reshape(rows_here, -1)
    new_momentum = leftover.reshape(1, rows_here, width)
    share = rows_here // replicas
    first_row = rep_index * share
    received = lax.all_to_all(
        values.reshape(replicas, share, values.shape[1]),
        "rep",
        split_axis=0,
        concat_axis=0,
        tiled=True,
    )
    summed = jnp.sum(received.astype(jnp.float32), axis=0)
    own_slots = lax.dynamic_slice_in_dim(positions, first_row, share, 0)
    update = decode(summed, own_slots, basis, KEEP, 1.0 / math.sqrt(replicas))
    return (new_momentum, update)


def solution(mesh):
    in_specs = (
        P(("rep", "fsdp"), None),
        P(("rep", "fsdp"), None),
        P("rep", "fsdp", None),
        P("fsdp", None),
    )
    out_specs = (P("rep", "fsdp", None), P(("fsdp", "rep"), None))
    return jax.shard_map(local, mesh=mesh, in_specs=in_specs, out_specs=out_specs, check_vma=False)
```

profile of v0, /device:TPU:1, one launch (start us, length us, event | category | flops | bytes accessed | tf_op | source)
XLA Modules:
  0.0 598.4 jit_solution(18424495697205149463)
XLA Ops:
  11.0 11.6 %all-to-all-start = ((bf16[192,8,640]{2,0,1:T(8,128)(2,1)}), bf16[192,8,640]{2,0,1:T(8,128)(2,1)S(1)}, u32[]{:S(2)}, u32[]{:S(2)}) async-start(bf16[192,8,640]{2,0,1:T(8,128)(2,1)} %bitcast.45), calls=%async_computation | async-start | bytes 3932160 | tf_op jit(solution)/shard_map/all_to_all | solution.py:56
  24.1 41.3 %all-to-all-done = bf16[192,8,640]{2,0,1:T(8,128)(2,1)S(1)} async-done(((bf16[192,8,640]{2,0,1:T(8,128)(2,1)}), bf16[192,8,640]{2,0,1:T(8,128)(2,1)S(1)}, u32[]{:S(2)}, u32[]{:S(2)}) %all-to-all-start) | async-done | bytes 1966112 | tf_op jit(solution)/shard_map/all_to_all | solution.py:56
  65.4 143.6 %all-gather.2.cloned.1.call-done = bf16[1536,2560]{1,0:T(8,128)(2,1)} async-done(((bf16[192,2560]{1,0:T(8,128)(2,1)}), bf16[1536,2560]{1,0:T(8,128)(2,1)}) %all-gather.2.cloned.1.call-update) | async-done | bytes 7864336 | tf_op jit(solution)/shard_map/all_gather | solution.py:61
  209.0 10.0 %bitcast_add_fusion = f32[640,2560]{1,0:T(8,128)} fusion(bf16[1,640,2560]{2,1,0:T(8,128)(2,1)} %param.8, bf16[1536,640]{1,0:T(8,128)(2,1)S(1)} %bitcast.44, bf16[1536,2560]{1,0:T(8,128)(2,1)} %all-gather.2.cloned.1.call-done), kind=kOutput, calls=%fused_computation.25 | convolution fusion | flops 5038080000 | bytes 19660800 | tf_op jit(solution)/shard_map/dot_general | solution.py:59
  219.0 340.1 %while.14 = (s32[]{:T(128)}, bf16[10,64,320]{2,1,0:T(8,128)(2,1)}, bf16[10,64,2560]{2,1,0:T(8,128)(2,1)}, s32[10,64,320]{2,1,0:T(8,128)S(1)}, f32[10,64,2560]{2,...) while((s32[]{:T(128)}, bf16[10,64,320]{2,1,0:T(8,128)(2,1)}, ...), condition=%wide.region_3.4_spmd.clone.clone, body=%wide.region_0.3_spmd.clone.clone.sunk | while | flops 259690496 | bytes 16558229 | solution.py:73
  223.8 8.3 %select_reduce_fusion.5 = bf16[64,40,8]{2,1,0:T(8,128)(2,1)S(1)} fusion(f32[64,40,64]{2,1,0:T(8,128)} %fusion.40, s32[64,40,8]{2,1,0:T(8,128)S(1)} %copy.93), kind=kLoop, calls=%fused_computation.2.clone.1 | loop fusion | flops 3911680 | bytes 778240 | tf_op jit(solution)/shard_map/while/body/eval_jaxpr/reduce_sum | solution.py:39
  233.9 15.4 %select_reduce_fusion.6 = f32[64,40,64]{2,1,0:T(8,128)S(1)} fusion(f32[64,40,8]{2,1,0:T(8,128)} %copy.96, s32[64,40,8]{2,1,0:T(8,128)S(1)} %copy.93), kind=kLoop, calls=%fused_computation.1.clone.1 | loop fusion | flops 3768320 | bytes 819200 | tf_op jit(solution)/shard_map/while/body/eval_jaxpr/reduce_sum | solution.py:29
  257.8 8.3 %select_reduce_fusion.5 = bf16[64,40,8]{2,1,0:T(8,128)(2,1)S(1)} fusion(f32[64,40,64]{2,1,0:T(8,128)} %fusion.40, s32[64,40,8]{2,1,0:T(8,128)S(1)} %copy.93), kind=kLoop, calls=%fused_computation.2.clone.1 | loop fusion | flops 3911680 | bytes 778240 | tf_op jit(solution)/shard_map/while/body/eval_jaxpr/reduce_sum | solution.py:39
  267.9 15.4 %select_reduce_fusion.6 = f32[64,40,64]{2,1,0:T(8,128)S(1)} fusion(f32[64,40,8]{2,1,0:T(8,128)} %copy.96, s32[64,40,8]{2,1,0:T(8,128)S(1)} %copy.93), kind=kLoop, calls=%fused_computation.1.clone.1 | loop fusion | flops 3768320 | bytes 819200 | tf_op jit(solution)/shard_map/while/body/eval_jaxpr/reduce_sum | solution.py:29
  291.8 8.3 %select_reduce_fusion.5 = bf16[64,40,8]{2,1,0:T(8,128)(2,1)S(1)} fusion(f32[64,40,64]{2,1,0:T(8,128)} %fusion.40, s32[64,40,8]{2,1,0:T(8,128)S(1)} %copy.93), kind=kLoop, calls=%fused_computation.2.clone.1 | loop fusion | flops 3911680 | bytes 778240 | tf_op jit(solution)/shard_map/while/body/eval_jaxpr/reduce_sum | solution.py:39
  301.9 15.4 %select_reduce_fusion.6 = f32[64,40,64]{2,1,0:T(8,128)S(1)} fusion(f32[64,40,8]{2,1,0:T(8,128)} %copy.96, s32[64,40,8]{2,1,0:T(8,128)S(1)} %copy.93), kind=kLoop, calls=%fused_computation.1.clone.1 | loop fusion | flops 3768320 | bytes 819200 | tf_op jit(solution)/shard_map/while/body/eval_jaxpr/reduce_sum | solution.py:29
  325.8 8.3 %select_reduce_fusion.5 = bf16[64,40,8]{2,1,0:T(8,128)(2,1)S(1)} fusion(f32[64,40,64]{2,1,0:T(8,128)} %fusion.40, s32[64,40,8]{2,1,0:T(8,128)S(1)} %copy.93), kind=kLoop, calls=%fused_computation.2.clone.1 | loop fusion | flops 3911680 | bytes 778240 | tf_op jit(solution)/shard_map/while/body/eval_jaxpr/reduce_sum | solution.py:39
  335.9 15.4 %select_reduce_fusion.6 = f32[64,40,64]{2,1,0:T(8,128)S(1)} fusion(f32[64,40,8]{2,1,0:T(8,128)} %copy.96, s32[64,40,8]{2,1,0:T(8,128)S(1)} %copy.93), kind=kLoop, calls=%fused_computation.1.clone.1 | loop fusion | flops 3768320 | bytes 819200 | tf_op jit(solution)/shard_map/while/body/eval_jaxpr/reduce_sum | solution.py:29
  359.8 8.3 %select_reduce_fusion.5 = bf16[64,40,8]{2,1,0:T(8,128)(2,1)S(1)} fusion(f32[64,40,64]{2,1,0:T(8,128)} %fusion.40, s32[64,40,8]{2,1,0:T(8,128)S(1)} %copy.93), kind=kLoop, calls=%fused_computation.2.clone.1 | loop fusion | flops 3911680 | bytes 778240 | tf_op jit(solution)/shard_map/while/body/eval_jaxpr/reduce_sum | solution.py:39
  369.9 15.4 %select_reduce_fusion.6 = f32[64,40,64]{2,1,0:T(8,128)S(1)} fusion(f32[64,40,8]{2,1,0:T(8,128)} %copy.96, s32[64,40,8]{2,1,0:T(8,128)S(1)} %copy.93), kind=kLoop, calls=%fused_computation.1.clone.1 | loop fusion | flops 3768320 | bytes 819200 | tf_op jit(solution)/shard_map/while/body/eval_jaxpr/reduce_sum | solution.py:29
  393.9 8.3 %select_reduce_fusion.5 = bf16[64,40,8]{2,1,0:T(8,128)(2,1)S(1)} fusion(f32[64,40,64]{2,1,0:T(8,128)} %fusion.40, s32[64,40,8]{2,1,0:T(8,128)S(1)} %copy.93), kind=kLoop, calls=%fused_computation.2.clone.1 | loop fusion | flops 3911680 | bytes 778240 | tf_op jit(solution)/shard_map/while/body/eval_jaxpr/reduce_sum | solution.py:39
  403.9 15.4 %select_reduce_fusion.6 = f32[64,40,64]{2,1,0:T(8,128)S(1)} fusion(f32[64,40,8]{2,1,0:T(8,128)} %copy.96, s32[64,40,8]{2,1,0:T(8,128)S(1)} %copy.93), kind=kLoop, calls=%fused_computation.1.clone.1 | loop fusion | flops 3768320 | bytes 819200 | tf_op jit(solution)/shard_map/while/body/eval_jaxpr/reduce_sum | solution.py:29
  427.9 8.3 %select_reduce_fusion.5 = bf16[64,40,8]{2,1,0:T(8,128)(2,1)S(1)} fusion(f32[64,40,64]{2,1,0:T(8,128)} %fusion.40, s32[64,40,8]{2,1,0:T(8,128)S(1)} %copy.93), kind=kLoop, calls=%fused_computation.2.clone.1 | loop fusion | flops 3911680 | bytes 778240 | tf_op jit(solution)/shard_map/while/body/eval_jaxpr/reduce_sum | solution.py:39
  437.9 15.4 %select_reduce_fusion.6 = f32[64,40,64]{2,1,0:T(8,128)S(1)} fusion(f32[64,40,8]{2,1,0:T(8,128)} %copy.96, s32[64,40,8]{2,1,0:T(8,128)S(1)} %copy.93), kind=kLoop, calls=%fused_computation.1.clone.1 | loop fusion | flops 3768320 | bytes 819200 | tf_op jit(solution)/shard_map/while/body/eval_jaxpr/reduce_sum | solution.py:29
  461.9 8.3 %select_reduce_fusion.5 = bf16[64,40,8]{2,1,0:T(8,128)(2,1)S(1)} fusion(f32[64,40,64]{2,1,0:T(8,128)} %fusion.40, s32[64,40,8]{2,1,0:T(8,128)S(1)} %copy.93), kind=kLoop, calls=%fused_computation.2.clone.1 | loop fusion | flops 3911680 | bytes 778240 | tf_op jit(solution)/shard_map/while/body/eval_jaxpr/reduce_sum | solution.py:39
  472.0 15.4 %select_reduce_fusion.6 = f32[64,40,64]{2,1,0:T(8,128)S(1)} fusion(f32[64,40,8]{2,1,0:T(8,128)} %copy.96, s32[64,40,8]{2,1,0:T(8,128)S(1)} %copy.93), kind=kLoop, calls=%fused_computation.1.clone.1 | loop fusion | flops 3768320 | bytes 819200 | tf_op jit(solution)/shard_map/while/body/eval_jaxpr/reduce_sum | solution.py:29
  506.0 15.4 %select_reduce_fusion.6 = f32[64,40,64]{2,1,0:T(8,128)S(1)} fusion(f32[64,40,8]{2,1,0:T(8,128)} %copy.96, s32[64,40,8]{2,1,0:T(8,128)S(1)} %copy.93), kind=kLoop, calls=%fused_computation.1.clone.1 | loop fusion | flops 3768320 | bytes 819200 | tf_op jit(solution)/shard_map/while/body/eval_jaxpr/reduce_sum | solution.py:29
  540.0 15.4 %select_reduce_fusion.6 = f32[64,40,64]{2,1,0:T(8,128)S(1)} fusion(f32[64,40,8]{2,1,0:T(8,128)} %copy.96, s32[64,40,8]{2,1,0:T(8,128)S(1)} %copy.93), kind=kLoop, calls=%fused_computation.1.clone.1 | loop fusion | flops 3768320 | bytes 819200 | tf_op jit(solution)/shard_map/while/body/eval_jaxpr/reduce_sum | solution.py:29
  568.1 16.8 %all-to-all-done.1 = bf16[32,20,320]{2,1,0:T(8,128)(2,1)S(1)} async-done(((bf16[32,20,320]{2,1,0:T(8,128)(2,1)}), bf16[32,20,320]{2,1,0:T(8,128)(2,1)S(1)}, u32[]{:S(2)}, u32[]{:S(2)}) %all-to-all-start.1) | async-done | bytes 409632 | tf_op jit(solution)/shard_map/all_to_all | solution.py:84
  (199 shorter events, 139.1 us)
Async XLA Ops:
  7.2 201.9 %all-gather.2.cloned.1.call-start = ((), (), s32[]{:S(2)}) async-start(), calls=%async_computation.2 | async-start | bytes 8847360 | tf_op jit(solution)/shard_map/all_gather | solution.py:61
  11.0 54.4 %all-to-all-start = ((bf16[192,8,640]{2,0,1:T(8,128)(2,1)}), bf16[192,8,640]{2,0,1:T(8,128)(2,1)S(1)}, u32[]{:S(2)}, u32[]{:S(2)}) async-start(bf16[192,8,640]{2,0,1:T(8,128)(2,1)} %bitcast.45), calls=%async_computation | async-start | bytes 3932160 | tf_op jit(solution)/shard_map/all_to_all | solution.py:56
  219.0 4.2 copy-start
  249.3 3.7 copy-start.1
  253.1 4.2 copy-start
  283.3 3.7 copy-start.1
  287.1 4.2 copy-start
  317.3 3.7 copy-start.1
  321.1 4.2 copy-start
  351.4 3.7 copy-start.1
  355.1 4.2 copy-start
  385.4 3.8 copy-start.1
  389.1 4.2 copy-start
  419.4 3.7 copy-start.1
  423.1 4.2 copy-start
  453.4 3.7 copy-start.1
  457.1 4.2 copy-start
  487.4 3.7 copy-start.1
  491.2 4.2 copy-start
  521.4 3.7 copy-start.1
  525.2 4.2 copy-start
  555.4 3.7 copy-start.1
  561.2 23.7 %all-to-all-start.1 = ((bf16[32,20,320]{2,1,0:T(8,128)(2,1)}), bf16[32,20,320]{2,1,0:T(8,128)(2,1)S(1)}, u32[]{:S(2)}, u32[]{:S(2)}) async-start(bf16[32,20,320]{2,1,0:T(8,128)(2,1)} %reshape_reshape.3), calls=%async_computation.1 | async-start | bytes 1179648 | tf_op jit(solution)/shard_map/all_to_all | solution.py:84
Sparse Core Ops, SparseCore 0:
  10.6 198.3 all-gather.1
where the time goes:
time: 600 us; the launch traced here: 598 us
  other arithmetic  242 us (40%)
  waiting for transfers between devices  202 us (34%)
  local copies, waits for them, and re-layouts  73 us (12%)
  matrix products  48.4 us (8%)
  starting transfers between devices  17.2 us (3%)
  between operations  14.1 us (2%)
    reduce_sum x11, other arithmetic, expand(): spread = jnp.sum(jnp.where(chosen, values[..., None], 0.0), axis=2)  159 us
    all_gather x1, waiting for transfers between devices, local(): lax.all_gather(cotangent, 'fsdp', axis=0, tiled=True)  144 us
    reduce_sum x10, other arithmetic, compress(): jnp.sum(jnp.where(chosen, coeffs[:, :, None, :], 0.0), axis=3)  83.3 us
    all_to_all x1, waiting for transfers between devices, local(): lax.all_to_all(tokens, 'fsdp', split_axis=1, concat_axis=0, tiled=True)  41.3 us
    dot_general x10, matrix products, compress(): jnp.einsum('rcj,kj->rck', spans, basis, precision=lax.Precision.HIGHEST)  23.7 us
    all_to_all x1, waiting for transfers between devices, local(): lax.all_to_all(values.reshape(replicas, share, values.shape[1]), 'rep', s...  16.8 us
    dynamic_slice x30, local copies, waits for them, and re-layouts, local(): lax.map(compress_block, (updated.reshape(block_count, block_rows, width),...  16 us
    dot_general x11, matrix products, expand(): jnp.einsum('rck,kj->rcj', spread, basis, precision=lax.Precision.HIGHEST)  14.8 us
  transfers between devices with their start and end apart: 3, of which 3 were waited for; matrix products, arithmetic and copies ran while one was open for 1% of the time, Pallas kernels for 0%

commit v1 on v0

v1 whole, which is shorter than its diff:
```python
import functools
import math

import jax
import jax.numpy as jnp
import numpy as np
from jax import lax
from jax.experimental import pallas as pl
from jax.experimental.pallas import tpu as pltpu
from jax.sharding import PartitionSpec as P

SPAN = 64
KEEP = 8
MOMENTUM_DECAY = 0.9
MESH = pl.DeviceIdType.MESH

REPLICAS = 32
ROWS = 640
WIDTH = 2560
BLOCK = 192
SLOTS = 8
PIECE = 256
PIECES = WIDTH // PIECE
GROUPS = 3
GROUP_ROWS = ROWS // 4
WINDOW = 32
AHEAD = 3


def block_bases():
    freqs = np.arange(SPAN, dtype=np.float64)[:, None]
    places = np.arange(SPAN, dtype=np.float64)[None, :]
    weights = np.where(freqs == 0.0, math.sqrt(1.0 / SPAN), math.sqrt(2.0 / SPAN))
    basis = (weights * np.cos(math.pi * (2.0 * places + 1.0) * freqs / (2.0 * SPAN))).astype(np.float32)
    inverse = np.kron(np.eye(PIECE // SPAN, dtype=np.float32), basis)
    out = []
    for matrix in (inverse.T, inverse):
        high = matrix.astype(jnp.bfloat16)
        low = (matrix - high.astype(np.float32)).astype(jnp.bfloat16)
        out += [high, low]
    return np.stack(out)


def split(value):
    high = value.astype(jnp.bfloat16)
    return high, (value - high.astype(jnp.float32)).astype(jnp.bfloat16)


def mm(a, b):
    return jnp.dot(a, b, preferred_element_type=jnp.float32)


def lane_gather(value, index):
    return jnp.take_along_axis(value, index, axis=1, mode="promise_in_bounds")


ZT, ZG = 0, 4
YT, YTP = 14, 17
YG, YGR = 20, 22
YP, YPR = 24, 24 + 2 * PIECES
A0 = 24 + 4 * PIECES
B0 = A0 + 3 * GROUPS
REMOTE = B0 + 7 * GROUPS


def kernel(
    tok, cot, mom, pos, bases, out, upd,
    tall, gall, relay, tt, mom_s, pos_s, mask_s, idx_s, gidx_s, out_s, upd_s, vals_f, vals_b, abuf, pbuf, bbuf,
    ss, rs, ls,
):
    rep = lax.axis_index("rep")
    f = lax.axis_index("fsdp")
    x, q = rep // 8, lax.rem(rep, 8)
    zh, y = f // 4, lax.rem(f, 4)

    def at_y(j):
        return (rep, zh * 4 + lax.rem(y + j, 4))

    partner = (rep, lax.rem(f + 4, 8))

    def at_x(j):
        return (lax.rem(x + j, 4) * 8 + q, f)

    def at_q(j):
        return (x * 8 + lax.rem(q + j, 8), f)

    def remote(src, dst, k, device):
        return pltpu.make_async_remote_copy(
            src_ref=src, dst_ref=dst, send_sem=ss.at[k], recv_sem=rs.at[k], device_id=device, device_id_type=MESH
        )

    def tok_cols(block):
        return tok.at[:, pl.ds(pl.multiple_of(block * ROWS, 128), ROWS)]

    def cols(t):
        return pl.ds(pl.multiple_of(t * PIECE, PIECE), PIECE)

    def z_tok(j):
        src = tok_cols((1 - zh) * 4 + lax.rem(y + j, 4))
        return remote(src, tall.at[4] if j == 0 else relay.at[j - 1], ZT + j, partner)

    def z_cot(t):
        return remote(cot.at[:, cols(t)], gall.at[4, :, cols(t)], ZG + t, partner)

    def y_tok(j):
        return remote(tok_cols(zh * 4 + lax.rem(y + j, 4)), tall.at[4 - j], YT + j - 1, at_y(j))

    def y_tok_partner(j):
        return remote(relay.at[j - 1], tall.at[8 - j], YTP + j - 1, at_y(j))

    def y_cot(way):
        return remote(cot, gall.at[3 - 2 * way], YG + way, at_y(1 + 2 * way))

    def y_cot_relay(way):
        half = pl.ds(96 * way, 96)
        return remote(gall.at[3 - 2 * way, half], gall.at[2, half], YGR + way, at_y(1 + 2 * way))

    def y_piece(t, way):
        return remote(gall.at[4, :, cols(t)], gall.at[7 - 2 * way, :, cols(t)], YP + 2 * t + way, at_y(1 + 2 * way))

    def y_piece_relay(t, way):
        half = pl.ds(96 * way, 96)
        return remote(
            gall.at[7 - 2 * way, half, cols(t)], gall.at[6, half, cols(t)], YPR + 2 * t + way, at_y(1 + 2 * way)
        )

    def rep_x(b, j):
        rows = pl.ds(pl.multiple_of(lax.rem(x + j, 4) * GROUP_ROWS, 32), GROUP_ROWS)
        return remote(vals_b.at[b, rows], abuf.at[b, j - 1], A0 + 3 * b + j - 1, at_x(j))

    def window(who):
        return pl.ds(pl.multiple_of(((5 * who) // 4) * 16, 16), WINDOW)

    def rep_q(b, j):
        rows = window(lax.rem(q + j, 8))
        return remote(pbuf.at[b, rows], bbuf.at[b, j - 1], B0 + 7 * b + j - 1, at_q(j))

    def local(src, dst, k):
        return pltpu.make_async_copy(src, dst, ls.at[k])

    locals_in = [
        local(pos, pos_s, 0),
        local(cot, gall.at[0], 1),
        local(tok_cols(f), tall.at[0], 2),
        local(mom, mom_s, 3),
    ]
    for copy in locals_in:
        copy.start()

    barrier = pltpu.get_barrier_semaphore()
    friends = [partner] + [at_y(j) for j in (1, 2, 3)] + [at_x(j) for j in (1, 2, 3)] + [at_q(j) for j in range(1, 8)]
    for friend in friends:
        pl.semaphore_signal(barrier, inc=1, device_id=friend, device_id_type=MESH)
    pl.semaphore_wait(barrier, len(friends))

    for j in (1, 2, 3):
        z_tok(j).start()
    for way in (0, 1):
        y_cot(way).start()
    for j in (1, 3, 2):
        y_tok(j).start()

    locals_in[0].wait()

    def lanes(rows):
        return lax.broadcasted_iota(jnp.int32, (rows, 128), 1)

    def position_blocks(p):
        return (p[:, 0:128], p[:, 128:256], p[:, 192:320])

    def blocks_of(b):
        return [(bb, 8 * b + bb) for bb in range(8)] if b < 2 else [(bb, 12 + bb) for bb in range(4, 8)]

    def prepare(i, carry):
        rows = pl.ds(pl.multiple_of(i * 32, 32), 32)
        lane = lanes(32)
        half = 8 * (lane // 64)
        inside = lax.rem(lane, 64)
        shift = 64 * lax.rem(lane // 8, 2)
        for b, block in enumerate(position_blocks(pos_s[rows, :])):
            idx_s[b, rows, :] = block + shift
            for bb, column in blocks_of(b):
                hit = jnp.zeros((32, 128), jnp.float32)
                for m in range(KEEP):
                    hit = jnp.where(lane_gather(block, half + (16 * bb + m)) == inside, 1.0, hit)
                mask_s[rows, column * 128 : column * 128 + 128] = hit.astype(jnp.bfloat16)
        return carry

    lax.fori_loop(0, ROWS // 32, prepare, 0)

    lane32 = lanes(WINDOW)
    half32 = 8 * (lane32 // 64)
    inside32 = lax.rem(lane32, 64)
    for b, block in enumerate(position_blocks(pos_s[window(rep), :])):
        for bb, column in blocks_of(b):
            found = jnp.full((WINDOW, 128), -1, jnp.int32)
            for m in range(KEEP):
                source = half32 + (16 * bb + m)
                found = jnp.where(lane_gather(block, source) == inside32, source, found)
            gidx_s[:, column * 128 : column * 128 + 128] = found

    z_tok(1).wait_recv()
    y_tok_partner(1).start()
    z_tok(0).start()
    for way in (0, 1):
        y_cot(way).wait_recv()
        y_cot_relay(way).start()
    z_tok(2).wait_recv()
    y_tok_partner(2).start()
    z_cot(0).start()
    z_tok(3).wait_recv()
    y_tok_partner(3).start()
    z_cot(1).start()

    def turn(pair):
        block = tall[2 * pair : 2 * pair + 2].reshape(2 * BLOCK, ROWS)
        tt[:, pair * 2 * BLOCK : (pair + 1) * 2 * BLOCK] = block.T

    for copy in locals_in[1:]:
        copy.wait()
    for j in (1, 2, 3):
        y_tok(j).wait_recv()
    turn(0)
    turn(1)
    z_tok(0).wait_recv()
    z_cot(2).start()
    for j in (1, 2, 3):
        y_tok_partner(j).wait_recv()
    turn(2)
    turn(3)
    for way in (0, 1):
        y_cot_relay(way).wait_recv()

    def compute(s):
        c = cols(s)
        gradient = mm(tt[...], gall[:, :, c].reshape(SLOTS * BLOCK, PIECE))
        updated = MOMENTUM_DECAY * mom_s[:, c].astype(jnp.float32) + gradient
        high, low = split(updated)
        coeffs = mm(high, bases[0]) + mm(low, bases[0]) + mm(high, bases[1])
        rounded = coeffs.astype(jnp.bfloat16)
        kept = rounded * mask_s[:, c]
        restored = mm(kept, bases[2]) + mm(kept, bases[3])
        out_s[s] = (updated - restored).astype(jnp.bfloat16)
        local(out_s.at[s], out.at[:, c], 4 + s).start()
        b = s // 4
        first = 2 * lax.rem(s, 4) + jnp.where(s >= 8, 4, 0)
        index = idx_s[b]
        values = vals_f[...]
        place = lanes(ROWS) // 16
        wide = rounded.astype(jnp.float32)
        for k in (0, 1):
            values = jnp.where(place == first + k, lane_gather(wide[:, k * 128 : k * 128 + 128], index), values)
        vals_f[...] = values

    def share(b):
        vals_b[b] = vals_f[...].astype(jnp.bfloat16)
        for j in (1, 2, 3):
            rep_x(b, j).start()

    def add_x(b):
        own = pl.ds(pl.multiple_of(x * GROUP_ROWS, 32), GROUP_ROWS)
        total = vals_b[b, own, :].astype(jnp.float32)
        for j in (1, 2, 3):
            rep_x(b, j).wait_recv()
            total = total + abuf[b, j - 1].astype(jnp.float32)
        pbuf[b] = total
        for j in range(1, 8):
            rep_q(b, j).start()

    def decode(b):
        total = pbuf[b, window(q), :]
        for j in range(1, 8):
            rep_q(b, j).wait_recv()
            total = total + bbuf[b, j - 1]
        parts = []
        for _, column in blocks_of(b):
            found = gidx_s[:, column * 128 : column * 128 + 128]
            parts.append(jnp.where(found >= 0, lane_gather(total, jnp.maximum(found, 0)), 0.0))
        spread = jnp.concatenate(
            [jnp.concatenate(parts[k : k + 2], axis=1) for k in range(0, len(parts), 2)], axis=0
        )
        high, low = split(spread)
        restored = mm(high, bases[2]) + mm(low, bases[2]) + mm(high, bases[3])
        restored = (restored * (1.0 / math.sqrt(REPLICAS))).astype(jnp.bfloat16)
        for k in range(len(parts) // 2):
            upd_s[:, b * 1024 + k * PIECE : b * 1024 + (k + 1) * PIECE] = restored[k * WINDOW : (k + 1) * WINDOW]

    vals_f[...] = jnp.zeros_like(vals_f)

    def step(t, carry):
        @pl.when(t < PIECES)
        def _():
            z_cot(t).wait_recv()
            for way in (0, 1):
                y_piece(t, way).start()

        @pl.when(t + AHEAD < PIECES)
        def _():
            z_cot(t + AHEAD).start()

        @pl.when((t >= 1) & (t <= PIECES))
        def _():
            for way in (0, 1):
                y_piece(t - 1, way).wait_recv()
                y_piece_relay(t - 1, way).start()

        @pl.when(t >= 2)
        def _():
            for way in (0, 1):
                y_piece_relay(t - 2, way).wait_recv()
            compute(t - 2)

        @pl.when(t == 5)
        def _():
            share(0)

        @pl.when(t == 7)
        def _():
            add_x(0)

        @pl.when(t == 9)
        def _():
            share(1)
            decode(0)

        return carry

    lax.fori_loop(0, PIECES + 2, step, 0)
    share(2)
    add_x(1)
    add_x(2)
    decode(1)
    decode(2)
    last = local(upd_s, upd, 4 + PIECES)
    last.start()

    for j in range(4):
        z_tok(j).wait_send()
    for j in (1, 2, 3):
        y_tok(j).wait_send()
        y_tok_partner(j).wait_send()
    for way in (0, 1):
        y_cot(way).wait_send()
        y_cot_relay(way).wait_send()

    def finish(t, carry):
        z_cot(t).wait_send()
        for way in (0, 1):
            y_piece(t, way).wait_send()
            y_piece_relay(t, way).wait_send()
        local(out_s.at[t], out.at[:, cols(t)], 4 + t).wait()
        return carry

    lax.fori_loop(0, PIECES, finish, 0)
    for b in range(GROUPS):
        for j in (1, 2, 3):
            rep_x(b, j).wait_send()
        for j in range(1, 8):
            rep_q(b, j).wait_send()
    last.wait()


def body(tokens, cotangent, momentum, positions):
    anywhere = pl.BlockSpec(memory_space=pl.ANY)
    bf16, f32, i32 = jnp.bfloat16, jnp.float32, jnp.int32
    new_momentum, update = pl.pallas_call(
        kernel,
        out_shape=(jax.ShapeDtypeStruct((ROWS, WIDTH), bf16), jax.ShapeDtypeStruct((WINDOW, WIDTH), bf16)),
        in_specs=[anywhere] * 4 + [pl.BlockSpec(memory_space=pltpu.VMEM)],
        out_specs=(anywhere, anywhere),
        scratch_shapes=[
            pltpu.VMEM((SLOTS, BLOCK, ROWS), bf16),
            pltpu.VMEM((SLOTS, BLOCK, WIDTH), bf16),
            pltpu.VMEM((3, BLOCK, ROWS), bf16),
            pltpu.VMEM((ROWS, SLOTS * BLOCK), bf16),
            pltpu.VMEM((ROWS, WIDTH), bf16),
            pltpu.VMEM((ROWS, WIDTH // SPAN * KEEP), i32),
            pltpu.VMEM((ROWS, WIDTH), bf16),
            pltpu.VMEM((GROUPS, ROWS, 128), i32),
            pltpu.VMEM((WINDOW, WIDTH), i32),
            pltpu.VMEM((PIECES, ROWS, PIECE), bf16),
            pltpu.VMEM((WINDOW, WIDTH), bf16),
            pltpu.VMEM((ROWS, 128), f32),
            pltpu.VMEM((GROUPS, ROWS, 128), bf16),
            pltpu.VMEM((GROUPS, 3, GROUP_ROWS, 128), bf16),
            pltpu.VMEM((GROUPS, GROUP_ROWS, 128), f32),
            pltpu.VMEM((GROUPS, 7, WINDOW, 128), f32),
            pltpu.SemaphoreType.DMA((REMOTE,)),
            pltpu.SemaphoreType.DMA((REMOTE,)),
            pltpu.SemaphoreType.DMA((5 + PIECES,)),
        ],
        compiler_params=pltpu.CompilerParams(
            collective_id=0, has_side_effects=True, vmem_limit_bytes=60 * 1024 * 1024
        ),
    )(tokens, cotangent, momentum.reshape(ROWS, WIDTH), positions, jnp.asarray(block_bases()))
    first = 4 * lax.rem(lax.axis_index("rep"), 4)
    update = lax.dynamic_slice_in_dim(update, first, ROWS // REPLICAS, 0)
    return new_momentum.reshape(1, ROWS, WIDTH), update


def solution(mesh):
    in_specs = (
        P(("rep", "fsdp"), None),
        P(("rep", "fsdp"), None),
        P("rep", "fsdp", None),
        P("fsdp", None),
    )
    out_specs = (P("rep", "fsdp", None), P(("fsdp", "rep"), None))
    return jax.shard_map(body, mesh=mesh, in_specs=in_specs, out_specs=out_specs, check_vma=False)
```

time: 600 us -> 134 us (0.22)
  other arithmetic: 242 us -> 0 us
  waiting for transfers between devices: 202 us -> 0 us
  Pallas kernels: 0 us -> 125 us
  local copies, waits for them, and re-layouts: 73 us -> 7.88 us
  matrix products: 48.4 us -> 0 us
  starting transfers between devices: 17.2 us -> 0 us
  between operations: 14.1 us -> 0.65 us
    reduce_sum x22 -> x0, other arithmetic: 242 us -> none  [the longest x11 159 us: expand(): spread = jnp.sum(jnp.where(chosen, values[..., None], 0.0), axis=2)]
    all_gather x1 -> x0, waiting for transfers between devices: 144 us -> none  [local(): lax.all_gather(cotangent, 'fsdp', axis=0, tiled=True)]
    pallas_call x0 -> x1, Pallas kernels: none -> 125 us  [body(): pl.pallas_call(kernel, out_shape=(jax.ShapeDtypeStruct((ROWS, WIDTH), bf1...]
    all_to_all x2 -> x0, waiting for transfers between devices: 58 us -> none  [the longest x1 41.3 us: local(): lax.all_to_all(tokens, 'fsdp', split_axis=1, concat_axis=0, tiled=True)]
    dot_general x22 -> x0, matrix products: 48.4 us -> none  [the longest x10 23.7 us: compress(): jnp.einsum('rcj,kj->rck', spans, basis, precision=lax.Precision.HIGHEST)]
    convert_element_type x31 -> x0, local copies, waits for them, and re-layouts: 22.2 us -> none  [the longest x10 13.3 us: compress(): restored = expand(values.astype(jnp.float32), chosen, basis)]
    all_to_all x2 -> x0, starting transfers between devices: 17.2 us -> none  [the longest x1 11.6 us: local(): lax.all_to_all(tokens, 'fsdp', split_axis=1, concat_axis=0, tiled=True)]
    dynamic_update_slice x30 -> x0, local copies, waits for them, and re-layouts: 14.7 us -> none  [local(): lax.map(compress_block, (updated.reshape(block_count, block_rows, width),...]
  transfers between devices with their start and end apart: 3 -> 0, of which waited for: 3 -> 0; matrix products, arithmetic and copies ran while one was open for 1% -> 0% of each run, Pallas kernels for 0% -> 0%
where the time goes in v1:
time: 134 us
  Pallas kernels  125 us (93%)
  local copies, waits for them, and re-layouts  7.88 us (6%)
    pallas_call x1, Pallas kernels, body(): pl.pallas_call(kernel, out_shape=(jax.ShapeDtypeStruct((ROWS, WIDTH), bf1...  125 us
    unnamed x2, local copies, waits for them, and re-layouts  6.27 us

profile of v1, /device:TPU:1, one launch (start us, length us, event | category | flops | bytes accessed | tf_op | source)
XLA Modules:
  0.0 133.6 jit_solution(15741011951229269445)
XLA Ops:
  0.6 2.4 %copy.7.pos = s32[640,320]{1,0:T(8,128)} copy(s32[640,320]{0,1:T(8,128)} %param.8) | data formatting | bytes 1638400 | tf_op args[3]
  3.1 125.1 %shard_map.68 = (bf16[640,2560]{1,0:T(8,128)(2,1)}, bf16[32,2560]{1,0:T(8,128)(2,1)}) custom-call(bf16[192,5120]{1,0:T(8,128)(2,1)} %tok.1, bf16[192,2560]{1,0:T(8,128)(2,1)} %cot.1, bf16[640,2560]{1,0:T(8,128)(2,1)} %bitcast.3, s32[640,320]{1,0:T(8,128)} %copy.7.pos, bf16[4,256,256]{2,1,0:T(8,128)(2,1)} %constant.17.clone.bases), custom_call_target="tpu_custom_call" | custom-call | tf_op jit(solution)/shard_map/pallas_call | solution.py:366
  128.1 1.6 %constant_dynamic-slice_fusion = bf16[20,2560]{1,0:T(8,128)(2,1)} fusion(bf16[32,2560]{1,0:T(8,128)(2,1)} %get-tuple-element.5, s32[]{:T(128)S(6)} %select_n.3), kind=kLoop, calls=%fused_computation | loop fusion | bytes 204804 | tf_op jit(solution)/shard_map/dynamic_slice | solution.py:397
  129.7 3.8 %copy.9 = bf16[1,640,2560]{2,1,0:T(8,128)(2,1)} copy(bf16[1,640,2560]{2,1,0:T(8,128)(2,1)} %bitcast.2) | data formatting | bytes 6553600

commit v2 on v1

--- a/solution.py
+++ b/solution.py
@@ -21,6 +21,8 @@
 SLOTS = 8
 PIECE = 256
 PIECES = WIDTH // PIECE
+WHOLE = PIECES - 1
+HALF = PIECE // 2
 GROUPS = 3
 GROUP_ROWS = ROWS // 4
 WINDOW = 32
@@ -54,18 +56,20 @@
     return jnp.take_along_axis(value, index, axis=1, mode="promise_in_bounds")
 
 
-ZT, ZG = 0, 4
-YT, YTP = 14, 17
-YG, YGR = 20, 22
-YP, YPR = 24, 24 + 2 * PIECES
-A0 = 24 + 4 * PIECES
+ZT, ZG, ZH = 0, 4, 4 + WHOLE
+YT = ZH + 2
+YTP, YG, YGR = YT + 3, YT + 6, YT + 8
+YP = YGR + 2
+YPR = YP + 2 * WHOLE
+YH = YPR + 2 * WHOLE
+A0 = YH + 6
 B0 = A0 + 3 * GROUPS
 REMOTE = B0 + 7 * GROUPS
 
 
 def kernel(
-    tok, cot, mom, pos, bases, out, upd,
-    tall, gall, relay, tt, mom_s, pos_s, mask_s, idx_s, gidx_s, out_s, upd_s, vals_f, vals_b, abuf, pbuf, bbuf,
+    tok, cot, mom, pos, consts, out, upd,
+    tall, gall, relay, tt, mom_s, pos_s, bases, mask_s, idx_s, gidx_s, vals_f, vals_b, abuf, pbuf, bbuf,
     ss, rs, ls,
 ):
     rep = lax.axis_index("rep")
@@ -102,6 +106,10 @@
     def z_cot(t):
         return remote(cot.at[:, cols(t)], gall.at[4, :, cols(t)], ZG + t, partner)
 
+    def z_half(h):
+        c = pl.ds(WHOLE * PIECE + h * HALF, HALF)
+        return remote(cot.at[:, c], gall.at[4, :, c], ZH + h, partner)
+
     def y_tok(j):
         return remote(tok_cols(zh * 4 + lax.rem(y + j, 4)), tall.at[4 - j], YT + j - 1, at_y(j))
 
@@ -124,6 +132,10 @@
             gall.at[7 - 2 * way, half, cols(t)], gall.at[6, half, cols(t)], YPR + 2 * t + way, at_y(1 + 2 * way)
         )
 
+    def y_half(h, j):
+        c = pl.ds(WHOLE * PIECE + h * HALF, HALF)
+        return remote(gall.at[4, :, c], gall.at[8 - j, :, c], YH + 3 * h + j - 1, at_y(j))
+
     def rep_x(b, j):
         rows = pl.ds(pl.multiple_of(lax.rem(x + j, 4) * GROUP_ROWS, 32), GROUP_ROWS)
         return remote(vals_b.at[b, rows], abuf.at[b, j - 1], A0 + 3 * b + j - 1, at_x(j))
@@ -143,6 +155,7 @@
         local(cot, gall.at[0], 1),
         local(tok_cols(f), tall.at[0], 2),
         local(mom, mom_s, 3),
+        local(consts, bases, 4),
     ]
     for copy in locals_in:
         copy.start()
@@ -159,26 +172,33 @@
         y_cot(way).start()
     for j in (1, 3, 2):
         y_tok(j).start()
+    z_tok(0).start()
+    for t in range(AHEAD):
+        z_cot(t).start()
 
     locals_in[0].wait()
 
     def lanes(rows):
         return lax.broadcasted_iota(jnp.int32, (rows, 128), 1)
 
-    def position_blocks(p):
-        return (p[:, 0:128], p[:, 128:256], p[:, 192:320])
+    def shift(rows):
+        return SPAN * lax.rem(lanes(rows) // KEEP, 2)
 
     def blocks_of(b):
         return [(bb, 8 * b + bb) for bb in range(8)] if b < 2 else [(bb, 12 + bb) for bb in range(4, 8)]
+
+    for b, first in enumerate((0, 128, 192)):
+        for i in range(ROWS // 128):
+            rows = slice(i * 128, (i + 1) * 128)
+            idx_s[b, rows, :] = pos_s[first : first + 128, rows].T + shift(128)
 
     def prepare(i, carry):
         rows = pl.ds(pl.multiple_of(i * 32, 32), 32)
         lane = lanes(32)
-        half = 8 * (lane // 64)
-        inside = lax.rem(lane, 64)
-        shift = 64 * lax.rem(lane // 8, 2)
-        for b, block in enumerate(position_blocks(pos_s[rows, :])):
-            idx_s[b, rows, :] = block + shift
+        half = KEEP * (lane // SPAN)
+        inside = lax.rem(lane, SPAN)
+        for b in range(GROUPS):
+            block = idx_s[b, rows, :] - shift(32)
             for bb, column in blocks_of(b):
                 hit = jnp.zeros((32, 128), jnp.float32)
                 for m in range(KEEP):
@@ -188,29 +208,25 @@
 
     lax.fori_loop(0, ROWS // 32, prepare, 0)
 
-    lane32 = lanes(WINDOW)
-    half32 = 8 * (lane32 // 64)
-    inside32 = lax.rem(lane32, 64)
-    for b, block in enumerate(position_blocks(pos_s[window(rep), :])):
+    upwards = lax.rem(WINDOW - 4 * lax.rem(rep, 4), WINDOW)
+    lane = lanes(WINDOW)
+    for b in range(GROUPS):
+        block = pltpu.roll(idx_s[b, window(rep), :] - shift(WINDOW), upwards, 0)
         for bb, column in blocks_of(b):
             found = jnp.full((WINDOW, 128), -1, jnp.int32)
             for m in range(KEEP):
-                source = half32 + (16 * bb + m)
-                found = jnp.where(lane_gather(block, source) == inside32, source, found)
+                source = KEEP * (lane // SPAN) + (16 * bb + m)
+                found = jnp.where(lane_gather(block, source) == lax.rem(lane, SPAN), source, found)
             gidx_s[:, column * 128 : column * 128 + 128] = found
 
     z_tok(1).wait_recv()
     y_tok_partner(1).start()
-    z_tok(0).start()
     for way in (0, 1):
         y_cot(way).wait_recv()
         y_cot_relay(way).start()
-    z_tok(2).wait_recv()
-    y_tok_partner(2).start()
-    z_cot(0).start()
-    z_tok(3).wait_recv()
-    y_tok_partner(3).start()
-    z_cot(1).start()
+    for j in (2, 3):
+        z_tok(j).wait_recv()
+        y_tok_partner(j).start()
 
     def turn(pair):
         block = tall[2 * pair : 2 * pair + 2].reshape(2 * BLOCK, ROWS)
@@ -223,13 +239,6 @@
     turn(0)
     turn(1)
     z_tok(0).wait_recv()
-    z_cot(2).start()
-    for j in (1, 2, 3):
-        y_tok_partner(j).wait_recv()
-    turn(2)
-    turn(3)
-    for way in (0, 1):
-        y_cot_relay(way).wait_recv()
 
     def compute(s):
         c = cols(s)
@@ -240,8 +249,7 @@
         rounded = coeffs.astype(jnp.bfloat16)
         kept = rounded * mask_s[:, c]
         restored = mm(kept, bases[2]) + mm(kept, bases[3])
-        out_s[s] = (updated - restored).astype(jnp.bfloat16)
-        local(out_s.at[s], out.at[:, c], 4 + s).start()
+        out[:, c] = (updated - restored).astype(jnp.bfloat16)
         b = s // 4
         first = 2 * lax.rem(s, 4) + jnp.where(s >= 8, 4, 0)
         index = idx_s[b]
@@ -263,15 +271,16 @@
         for j in (1, 2, 3):
             rep_x(b, j).wait_recv()
             total = total + abuf[b, j - 1].astype(jnp.float32)
-        pbuf[b] = total
+        pbuf[b] = total.astype(jnp.bfloat16)
         for j in range(1, 8):
             rep_q(b, j).start()
 
     def decode(b):
-        total = pbuf[b, window(q), :]
+        total = pbuf[b, window(q), :].astype(jnp.float32)
         for j in range(1, 8):
             rep_q(b, j).wait_recv()
-            total = total + bbuf[b, j - 1]
+            total = total + bbuf[b, j - 1].astype(jnp.float32)
+        total = pltpu.roll(total, upwards, 0)
         parts = []
         for _, column in blocks_of(b):
             found = gidx_s[:, column * 128 : column * 128 + 128]
@@ -283,45 +292,88 @@
         restored = mm(high, bases[2]) + mm(low, bases[2]) + mm(high, bases[3])
         restored = (restored * (1.0 / math.sqrt(REPLICAS))).astype(jnp.bfloat16)
         for k in range(len(parts) // 2):
-            upd_s[:, b * 1024 + k * PIECE : b * 1024 + (k + 1) * PIECE] = restored[k * WINDOW : (k + 1) * WINDOW]
+            c = slice(b * 1024 + k * PIECE, b * 1024 + (k + 1) * PIECE)
+            upd[:, c] = restored[k * WINDOW : k * WINDOW + ROWS // REPLICAS]
 
     vals_f[...] = jnp.zeros_like(vals_f)
 
     def step(t, carry):
-        @pl.when(t < PIECES)
+        @pl.when(t < WHOLE)
         def _():
             z_cot(t).wait_recv()
             for way in (0, 1):
                 y_piece(t, way).start()
 
-        @pl.when(t + AHEAD < PIECES)
+        @pl.when(t + AHEAD < WHOLE)
         def _():
             z_cot(t + AHEAD).start()
 
-        @pl.when((t >= 1) & (t <= PIECES))
+        @pl.when(t + AHEAD == WHOLE)
+        def _():
+            z_half(0).start()
+            z_half(1).start()
+
+        @pl.when(t == WHOLE)
+        def _():
+            z_half(0).wait_recv()
+            for j in (1, 3, 2):
+                y_half(0, j).start()
+
+        @pl.when((t >= 1) & (t <= WHOLE))
         def _():
             for way in (0, 1):
                 y_piece(t - 1, way).wait_recv()
                 y_piece_relay(t - 1, way).start()
 
-        @pl.when(t >= 2)
-        def _():
+        @pl.when(t == WHOLE)
+        def _():
+            z_half(1).wait_recv()
+            for j in (1, 3, 2):
+                y_half(1, j).start()
+
+        @pl.when(t == 2)
+        def _():
+            for j in (1, 2, 3):
+                y_tok_partner(j).wait_recv()
+            turn(2)
+            turn(3)
             for way in (0, 1):
-                y_piece_relay(t - 2, way).wait_recv()
-            compute(t - 2)
+                y_cot_relay(way).wait_recv()
+
+        def finish_piece(s, inner):
+            @pl.when(s < WHOLE)
+            def _():
+                for way in (0, 1):
+                    y_piece_relay(s, way).wait_recv()
+
+            @pl.when(s == WHOLE)
+            def _():
+                for h in (0, 1):
+                    for j in (1, 2, 3):
+                        y_half(h, j).wait_recv()
+
+            compute(s)
+            return inner
+
+        @pl.when(t >= 3)
+        def _():
+            lax.fori_loop(jnp.where(t == 3, 0, t - 2), t - 1, finish_piece, 0)
 
         @pl.when(t == 5)
         def _():
             share(0)
 
-        @pl.when(t == 7)
+        @pl.when(t == 6)
         def _():
             add_x(0)
 
+        @pl.when(t == 8)
+        def _():
+            decode(0)
+
         @pl.when(t == 9)
         def _():
             share(1)
-            decode(0)
 
         return carry
 
@@ -331,8 +383,6 @@
     add_x(2)
     decode(1)
     decode(2)
-    last = local(upd_s, upd, 4 + PIECES)
-    last.start()
 
     for j in range(4):
         z_tok(j).wait_send()
@@ -348,53 +398,56 @@
         for way in (0, 1):
             y_piece(t, way).wait_send()
             y_piece_relay(t, way).wait_send()
-        local(out_s.at[t], out.at[:, cols(t)], 4 + t).wait()
         return carry
 
-    lax.fori_loop(0, PIECES, finish, 0)
+    lax.fori_loop(0, WHOLE, finish, 0)
+    for h in (0, 1):
+        z_half(h).wait_send()
+        for j in (1, 2, 3):
+            y_half(h, j).wait_send()
     for b in range(GROUPS):
         for j in (1, 2, 3):
             rep_x(b, j).wait_send()
         for j in range(1, 8):
             rep_q(b, j).wait_send()
-    last.wait()
 
 
 def body(tokens, cotangent, momentum, positions):
     anywhere = pl.BlockSpec(memory_space=pl.ANY)
+    near = pl.BlockSpec(memory_space=pltpu.VMEM)
     bf16, f32, i32 = jnp.bfloat16, jnp.float32, jnp.int32
     new_momentum, update = pl.pallas_call(
         kernel,
-        out_shape=(jax.ShapeDtypeStruct((ROWS, WIDTH), bf16), jax.ShapeDtypeStruct((WINDOW, WIDTH), bf16)),
-        in_specs=[anywhere] * 4 + [pl.BlockSpec(memory_space=pltpu.VMEM)],
-        out_specs=(anywhere, anywhere),
+        out_shape=(
+            pltpu.VMEM((ROWS, WIDTH), bf16),
+            pltpu.VMEM((ROWS // REPLICAS, WIDTH), bf16),
+        ),
+        in_specs=[anywhere] * 5,
+        out_specs=(near, near),
         scratch_shapes=[
             pltpu.VMEM((SLOTS, BLOCK, ROWS), bf16),
             pltpu.VMEM((SLOTS, BLOCK, WIDTH), bf16),
             pltpu.VMEM((3, BLOCK, ROWS), bf16),
             pltpu.VMEM((ROWS, SLOTS * BLOCK), bf16),
             pltpu.VMEM((ROWS, WIDTH), bf16),
-            pltpu.VMEM((ROWS, WIDTH // SPAN * KEEP), i32),
+            pltpu.VMEM((WIDTH // SPAN * KEEP, ROWS), i32),
+            pltpu.VMEM((4, PIECE, PIECE), bf16),
             pltpu.VMEM((ROWS, WIDTH), bf16),
             pltpu.VMEM((GROUPS, ROWS, 128), i32),
             pltpu.VMEM((WINDOW, WIDTH), i32),
-            pltpu.VMEM((PIECES, ROWS, PIECE), bf16),
-            pltpu.VMEM((WINDOW, WIDTH), bf16),
             pltpu.VMEM((ROWS, 128), f32),
             pltpu.VMEM((GROUPS, ROWS, 128), bf16),
             pltpu.VMEM((GROUPS, 3, GROUP_ROWS, 128), bf16),
-            pltpu.VMEM((GROUPS, GROUP_ROWS, 128), f32),
-            pltpu.VMEM((GROUPS, 7, WINDOW, 128), f32),
+            pltpu.VMEM((GROUPS, GROUP_ROWS, 128), bf16),
+            pltpu.VMEM((GROUPS, 7, WINDOW, 128), bf16),
             pltpu.SemaphoreType.DMA((REMOTE,)),
             pltpu.SemaphoreType.DMA((REMOTE,)),
-            pltpu.SemaphoreType.DMA((5 + PIECES,)),
+            pltpu.SemaphoreType.DMA((5,)),
         ],
         compiler_params=pltpu.CompilerParams(
-            collective_id=0, has_side_effects=True, vmem_limit_bytes=60 * 1024 * 1024
+            collective_id=0, has_side_effects=True, vmem_limit_bytes=56 * 1024 * 1024
         ),
-    )(tokens, cotangent, momentum.reshape(ROWS, WIDTH), positions, jnp.asarray(block_bases()))
-    first = 4 * lax.rem(lax.axis_index("rep"), 4)
-    update = lax.dynamic_slice_in_dim(update, first, ROWS // REPLICAS, 0)
+    )(tokens, cotangent, momentum.reshape(ROWS, WIDTH), positions.T, jnp.asarray(block_bases()))
     return new_momentum.reshape(1, ROWS, WIDTH), update
 
 

time: 134 us -> 126 us (0.940)
  local copies, waits for them, and re-layouts: 7.88 us -> 2.36 us
  Pallas kernels: 125 us -> 123 us
    unnamed x2, local copies, waits for them, and re-layouts: 6.27 us -> 2.36 us
    pallas_call x1, Pallas kernels: 125 us -> 123 us  [body(): pl.pallas_call(kernel, out_shape=(pltpu.VMEM((ROWS, WIDTH), bf16), pltpu....]
    dynamic_slice x1 -> x0, local copies, waits for them, and re-layouts: 1.61 us -> none  [body(): update = lax.dynamic_slice_in_dim(update, first, ROWS // REPLICAS, 0)]
where the time goes in v2:
time: 126 us
  Pallas kernels  123 us (98%)
  local copies, waits for them, and re-layouts  2.36 us (2%)
    pallas_call x1, Pallas kernels, body(): pl.pallas_call(kernel, out_shape=(pltpu.VMEM((ROWS, WIDTH), bf16), pltpu....  123 us

profile of v2, /device:TPU:1, one launch (start us, length us, event | category | flops | bytes accessed | tf_op | source)
XLA Modules:
  0.0 125.8 jit_solution(15515387721678729077)
XLA Ops:
  0.6 122.8 %shard_map.68 = (bf16[640,2560]{1,0:T(8,128)(2,1)S(1)}, bf16[20,2560]{1,0:T(8,128)(2,1)S(1)}) custom-call(bf16[192,5120]{1,0:T(8,128)(2,1)} %tok.1, bf16[192,2560]{1,0:T(8,128)(2,1)} %cot.1, bf16[640,2560]{1,0:T(8,128)(2,1)} %bitcast.4, s32[320,640]{1,0:T(8,128)} %bitcast.5, bf16[4,256,256]{2,1,0:T(8,128)(2,1)} %constant.2.clone.consts), custom_call_target="tpu_custom_call" | custom-call | tf_op jit(solution)/shard_map/pallas_call | solution.py:419
  123.4 1.7 %copy.9 = bf16[1,640,2560]{2,1,0:T(8,128)(2,1)} copy(bf16[1,640,2560]{2,1,0:T(8,128)(2,1)S(1)} %bitcast.3) | data formatting | bytes 6553600
  125.1 0.6 copy.10

commit v3 on v2

--- a/solution.py
+++ b/solution.py
@@ -193,31 +193,32 @@
             idx_s[b, rows, :] = pos_s[first : first + 128, rows].T + shift(128)
 
     def prepare(i, carry):
-        rows = pl.ds(pl.multiple_of(i * 32, 32), 32)
-        lane = lanes(32)
+        rows = pl.ds(pl.multiple_of(i * 16, 16), 16)
+        lane = lanes(16)
         half = KEEP * (lane // SPAN)
         inside = lax.rem(lane, SPAN)
         for b in range(GROUPS):
-            block = idx_s[b, rows, :] - shift(32)
+            block = idx_s[b, rows, :] - shift(16)
             for bb, column in blocks_of(b):
-                hit = jnp.zeros((32, 128), jnp.float32)
+                hit = jnp.zeros((16, 128), jnp.float32)
                 for m in range(KEEP):
                     hit = jnp.where(lane_gather(block, half + (16 * bb + m)) == inside, 1.0, hit)
                 mask_s[rows, column * 128 : column * 128 + 128] = hit.astype(jnp.bfloat16)
         return carry
 
-    lax.fori_loop(0, ROWS // 32, prepare, 0)
+    lax.fori_loop(0, ROWS // 16, prepare, 0)
 
     upwards = lax.rem(WINDOW - 4 * lax.rem(rep, 4), WINDOW)
     lane = lanes(WINDOW)
+    gidx_s[2, :, 0:512] = jnp.full((WINDOW, 512), -1, jnp.int32)
     for b in range(GROUPS):
         block = pltpu.roll(idx_s[b, window(rep), :] - shift(WINDOW), upwards, 0)
-        for bb, column in blocks_of(b):
+        for bb, _ in blocks_of(b):
             found = jnp.full((WINDOW, 128), -1, jnp.int32)
             for m in range(KEEP):
                 source = KEEP * (lane // SPAN) + (16 * bb + m)
                 found = jnp.where(lane_gather(block, source) == lax.rem(lane, SPAN), source, found)
-            gidx_s[:, column * 128 : column * 128 + 128] = found
+            gidx_s[b, :, bb * 128 : bb * 128 + 128] = found
 
     z_tok(1).wait_recv()
     y_tok_partner(1).start()
@@ -282,8 +283,8 @@
             total = total + bbuf[b, j - 1].astype(jnp.float32)
         total = pltpu.roll(total, upwards, 0)
         parts = []
-        for _, column in blocks_of(b):
-            found = gidx_s[:, column * 128 : column * 128 + 128]
+        for bb in range(8):
+            found = gidx_s[b, :, bb * 128 : bb * 128 + 128]
             parts.append(jnp.where(found >= 0, lane_gather(total, jnp.maximum(found, 0)), 0.0))
         spread = jnp.concatenate(
             [jnp.concatenate(parts[k : k + 2], axis=1) for k in range(0, len(parts), 2)], axis=0
@@ -291,9 +292,15 @@
         high, low = split(spread)
         restored = mm(high, bases[2]) + mm(low, bases[2]) + mm(high, bases[3])
         restored = (restored * (1.0 / math.sqrt(REPLICAS))).astype(jnp.bfloat16)
-        for k in range(len(parts) // 2):
-            c = slice(b * 1024 + k * PIECE, b * 1024 + (k + 1) * PIECE)
-            upd[:, c] = restored[k * WINDOW : k * WINDOW + ROWS // REPLICAS]
+        rows = [restored[k * WINDOW : k * WINDOW + ROWS // REPLICAS] for k in range(4)]
+
+        @pl.when(b < 2)
+        def _():
+            for k in (0, 1):
+                upd[:, cols(4 * b + k)] = rows[k]
+
+        for k in (2, 3):
+            upd[:, cols(jnp.where(b < 2, 4 * b, 6) + k)] = rows[k]
 
     vals_f[...] = jnp.zeros_like(vals_f)
 
@@ -355,34 +362,25 @@
             compute(s)
             return inner
 
-        @pl.when(t >= 3)
+        @pl.when((t >= 3) & (t <= PIECES + 1))
         def _():
             lax.fori_loop(jnp.where(t == 3, 0, t - 2), t - 1, finish_piece, 0)
 
-        @pl.when(t == 5)
-        def _():
-            share(0)
-
-        @pl.when(t == 6)
-        def _():
-            add_x(0)
-
-        @pl.when(t == 8)
-        def _():
-            decode(0)
-
-        @pl.when(t == 9)
-        def _():
-            share(1)
+        @pl.when((t == 5) | (t == 9) | (t == 11))
+        def _():
+            share(jnp.where(t == 5, 0, jnp.where(t == 9, 1, 2)))
+
+        @pl.when((t == 6) | (t == 12) | (t == 13))
+        def _():
+            add_x(jnp.where(t == 6, 0, t - 11))
+
+        @pl.when((t == 8) | (t == 14) | (t == 15))
+        def _():
+            decode(jnp.where(t == 8, 0, t - 13))
 
         return carry
 
-    lax.fori_loop(0, PIECES + 2, step, 0)
-    share(2)
-    add_x(1)
-    add_x(2)
-    decode(1)
-    decode(2)
+    lax.fori_loop(0, PIECES + 6, step, 0)
 
     for j in range(4):
         z_tok(j).wait_send()
@@ -434,7 +432,7 @@
             pltpu.VMEM((4, PIECE, PIECE), bf16),
             pltpu.VMEM((ROWS, WIDTH), bf16),
             pltpu.VMEM((GROUPS, ROWS, 128), i32),
-            pltpu.VMEM((WINDOW, WIDTH), i32),
+            pltpu.VMEM((GROUPS, WINDOW, 1024), i32),
             pltpu.VMEM((ROWS, 128), f32),
             pltpu.VMEM((GROUPS, ROWS, 128), bf16),
             pltpu.VMEM((GROUPS, 3, GROUP_ROWS, 128), bf16),

time: 126 us -> 124 us (0.984)
  Pallas kernels: 123 us -> 121 us
    pallas_call x1, Pallas kernels: 123 us -> 121 us  [body(): pl.pallas_call(kernel, out_shape=(pltpu.VMEM((ROWS, WIDTH), bf16), pltpu....]
where the time goes in v3:
time: 124 us
  Pallas kernels  121 us (98%)
  local copies, waits for them, and re-layouts  2.36 us (2%)
    pallas_call x1, Pallas kernels, body(): pl.pallas_call(kernel, out_shape=(pltpu.VMEM((ROWS, WIDTH), bf16), pltpu....  121 us

profile of v3, /device:TPU:1, one launch (start us, length us, event | category | flops | bytes accessed | tf_op | source)
XLA Modules:
  0.0 123.6 jit_solution(3241515639408587384)
XLA Ops:
  0.6 120.6 %shard_map.68 = (bf16[640,2560]{1,0:T(8,128)(2,1)S(1)}, bf16[20,2560]{1,0:T(8,128)(2,1)S(1)}) custom-call(bf16[192,5120]{1,0:T(8,128)(2,1)} %tok.1, bf16[192,2560]{1,0:T(8,128)(2,1)} %cot.1, bf16[640,2560]{1,0:T(8,128)(2,1)} %bitcast.4, s32[320,640]{1,0:T(8,128)} %bitcast.5, bf16[4,256,256]{2,1,0:T(8,128)(2,1)} %constant.2.clone.consts), custom_call_target="tpu_custom_call" | custom-call | tf_op jit(solution)/shard_map/pallas_call | solution.py:417
  121.3 1.7 %copy.9 = bf16[1,640,2560]{2,1,0:T(8,128)(2,1)} copy(bf16[1,640,2560]{2,1,0:T(8,128)(2,1)S(1)} %bitcast.3) | data formatting | bytes 6553600
  123.0 0.6 copy.10

commit v4 on v3

--- a/solution.py
+++ b/solution.py
@@ -166,13 +166,12 @@
         pl.semaphore_signal(barrier, inc=1, device_id=friend, device_id_type=MESH)
     pl.semaphore_wait(barrier, len(friends))
 
-    for j in (1, 2, 3):
+    for j in (1, 2, 3, 0):
         z_tok(j).start()
     for way in (0, 1):
         y_cot(way).start()
     for j in (1, 3, 2):
         y_tok(j).start()
-    z_tok(0).start()
     for t in range(AHEAD):
         z_cot(t).start()
 
@@ -249,8 +248,6 @@
         coeffs = mm(high, bases[0]) + mm(low, bases[0]) + mm(high, bases[1])
         rounded = coeffs.astype(jnp.bfloat16)
         kept = rounded * mask_s[:, c]
-        restored = mm(kept, bases[2]) + mm(kept, bases[3])
-        out[:, c] = (updated - restored).astype(jnp.bfloat16)
         b = s // 4
         first = 2 * lax.rem(s, 4) + jnp.where(s >= 8, 4, 0)
         index = idx_s[b]
@@ -260,6 +257,13 @@
         for k in (0, 1):
             values = jnp.where(place == first + k, lane_gather(wide[:, k * 128 : k * 128 + 128], index), values)
         vals_f[...] = values
+
+        @pl.when((s == 3) | (s == 7) | (s == 9))
+        def _():
+            share(b)
+
+        restored = mm(kept, bases[2]) + mm(kept, bases[3])
+        out[:, c] = (updated - restored).astype(jnp.bfloat16)
 
     def share(b):
         vals_b[b] = vals_f[...].astype(jnp.bfloat16)
@@ -365,10 +369,6 @@
         @pl.when((t >= 3) & (t <= PIECES + 1))
         def _():
             lax.fori_loop(jnp.where(t == 3, 0, t - 2), t - 1, finish_piece, 0)
-
-        @pl.when((t == 5) | (t == 9) | (t == 11))
-        def _():
-            share(jnp.where(t == 5, 0, jnp.where(t == 9, 1, 2)))
 
         @pl.when((t == 6) | (t == 12) | (t == 13))
         def _():

time: 124 us -> 126 us (1.016)
  Pallas kernels: 121 us -> 123 us
    pallas_call x1, Pallas kernels: 121 us -> 123 us  [body(): pl.pallas_call(kernel, out_shape=(pltpu.VMEM((ROWS, WIDTH), bf16), pltpu....]
where the time goes in v4:
time: 126 us
  Pallas kernels  123 us (98%)
  local copies, waits for them, and re-layouts  2.36 us (2%)
    pallas_call x1, Pallas kernels, body(): pl.pallas_call(kernel, out_shape=(pltpu.VMEM((ROWS, WIDTH), bf16), pltpu....  123 us

profile of v4, /device:TPU:1, one launch (start us, length us, event | category | flops | bytes accessed | tf_op | source)
XLA Modules:
  0.0 125.9 jit_solution(16534365587931145641)
XLA Ops:
  0.6 122.9 %shard_map.68 = (bf16[640,2560]{1,0:T(8,128)(2,1)S(1)}, bf16[20,2560]{1,0:T(8,128)(2,1)S(1)}) custom-call(bf16[192,5120]{1,0:T(8,128)(2,1)} %tok.1, bf16[192,2560]{1,0:T(8,128)(2,1)} %cot.1, bf16[640,2560]{1,0:T(8,128)(2,1)} %bitcast.4, s32[320,640]{1,0:T(8,128)} %bitcast.5, bf16[4,256,256]{2,1,0:T(8,128)(2,1)} %constant.2.clone.consts), custom_call_target="tpu_custom_call" | custom-call | tf_op jit(solution)/shard_map/pallas_call | solution.py:417
  123.6 1.7 %copy.9 = bf16[1,640,2560]{2,1,0:T(8,128)(2,1)} copy(bf16[1,640,2560]{2,1,0:T(8,128)(2,1)S(1)} %bitcast.3) | data formatting | bytes 6553600
  125.3 0.6 copy.10

commit v5 on v3

--- a/solution.py
+++ b/solution.py
@@ -69,7 +69,7 @@
 
 def kernel(
     tok, cot, mom, pos, consts, out, upd,
-    tall, gall, relay, tt, mom_s, pos_s, bases, mask_s, idx_s, gidx_s, vals_f, vals_b, abuf, pbuf, bbuf,
+    tall, gall, relay, tt, mom_s, pos_s, bases, mask_s, idx_s, gidx_s, updated_s, vals_f, vals_b, abuf, pbuf, bbuf,
     ss, rs, ls,
 ):
     rep = lax.axis_index("rep")
@@ -244,22 +244,29 @@
     def compute(s):
         c = cols(s)
         gradient = mm(tt[...], gall[:, :, c].reshape(SLOTS * BLOCK, PIECE))
-        updated = MOMENTUM_DECAY * mom_s[:, c].astype(jnp.float32) + gradient
-        high, low = split(updated)
-        coeffs = mm(high, bases[0]) + mm(low, bases[0]) + mm(high, bases[1])
-        rounded = coeffs.astype(jnp.bfloat16)
-        kept = rounded * mask_s[:, c]
-        restored = mm(kept, bases[2]) + mm(kept, bases[3])
-        out[:, c] = (updated - restored).astype(jnp.bfloat16)
+        updated_s[...] = MOMENTUM_DECAY * mom_s[:, c].astype(jnp.float32) + gradient
         b = s // 4
         first = 2 * lax.rem(s, 4) + jnp.where(s >= 8, 4, 0)
-        index = idx_s[b]
-        values = vals_f[...]
-        place = lanes(ROWS) // 16
-        wide = rounded.astype(jnp.float32)
-        for k in (0, 1):
-            values = jnp.where(place == first + k, lane_gather(wide[:, k * 128 : k * 128 + 128], index), values)
-        vals_f[...] = values
+        place = lanes(ROWS // 2) // 16
+
+        def transform(i, carry):
+            rows = pl.ds(pl.multiple_of(i * (ROWS // 2), ROWS // 2), ROWS // 2)
+            updated = updated_s[rows, :]
+            high, low = split(updated)
+            coeffs = mm(high, bases[0]) + mm(low, bases[0]) + mm(high, bases[1])
+            rounded = coeffs.astype(jnp.bfloat16)
+            kept = rounded * mask_s[rows, c]
+            restored = mm(kept, bases[2]) + mm(kept, bases[3])
+            out[rows, c] = (updated - restored).astype(jnp.bfloat16)
+            index = idx_s[b, rows, :]
+            values = vals_f[rows, :]
+            wide = rounded.astype(jnp.float32)
+            for k in (0, 1):
+                values = jnp.where(place == first + k, lane_gather(wide[:, k * 128 : k * 128 + 128], index), values)
+            vals_f[rows, :] = values
+            return carry
+
+        lax.fori_loop(0, 2, transform, 0)
 
     def share(b):
         vals_b[b] = vals_f[...].astype(jnp.bfloat16)
@@ -403,11 +410,14 @@
         z_half(h).wait_send()
         for j in (1, 2, 3):
             y_half(h, j).wait_send()
-    for b in range(GROUPS):
+    def shared(b, carry):
         for j in (1, 2, 3):
             rep_x(b, j).wait_send()
         for j in range(1, 8):
             rep_q(b, j).wait_send()
+        return carry
+
+    lax.fori_loop(0, GROUPS, shared, 0)
 
 
 def body(tokens, cotangent, momentum, positions):
@@ -433,6 +443,7 @@
             pltpu.VMEM((ROWS, WIDTH), bf16),
             pltpu.VMEM((GROUPS, ROWS, 128), i32),
             pltpu.VMEM((GROUPS, WINDOW, 1024), i32),
+            pltpu.VMEM((ROWS, PIECE), f32),
             pltpu.VMEM((ROWS, 128), f32),
             pltpu.VMEM((GROUPS, ROWS, 128), bf16),
             pltpu.VMEM((GROUPS, 3, GROUP_ROWS, 128), bf16),

time: 124 us -> 124 us (level)
  no operation moved by 1% of the time
where the time goes in v5:
time: 124 us
  Pallas kernels  121 us (98%)
  local copies, waits for them, and re-layouts  2.36 us (2%)
    pallas_call x1, Pallas kernels, body(): pl.pallas_call(kernel, out_shape=(pltpu.VMEM((ROWS, WIDTH), bf16), pltpu....  121 us

profile of v5, /device:TPU:1, one launch (start us, length us, event | category | flops | bytes accessed | tf_op | source)
XLA Modules:
  0.0 123.6 jit_solution(13593507215406525259)
XLA Ops:
  0.6 120.6 %shard_map.68 = (bf16[640,2560]{1,0:T(8,128)(2,1)S(1)}, bf16[20,2560]{1,0:T(8,128)(2,1)S(1)}) custom-call(bf16[192,5120]{1,0:T(8,128)(2,1)} %tok.1, bf16[192,2560]{1,0:T(8,128)(2,1)} %cot.1, bf16[640,2560]{1,0:T(8,128)(2,1)} %bitcast.4, s32[320,640]{1,0:T(8,128)} %bitcast.5, bf16[4,256,256]{2,1,0:T(8,128)(2,1)} %constant.2.clone.consts), custom_call_target="tpu_custom_call" | custom-call | tf_op jit(solution)/shard_map/pallas_call | solution.py:427
  121.2 1.7 %copy.9 = bf16[1,640,2560]{2,1,0:T(8,128)(2,1)} copy(bf16[1,640,2560]{2,1,0:T(8,128)(2,1)S(1)} %bitcast.3) | data formatting | bytes 6553600
  122.9 0.6 copy.10
